TPU v7x, 256 devices: a whole 4x4x8 slice. The times are simulated.
256 devices in a mesh: prow: 8 (over x, core), pcol: 32 (over z, y).
Axes of the slice: x: 4, y: 4, z: 8, core: 2. Of those that a mesh axis runs over, the one named last changes fastest.
Arguments:
- rhs: float32 [64, 65536], P(None, 'pcol'), may hold values from -6 to 6
- pivots: int32 [65536], P('pcol'), may hold values from 0 to 65535, as said below
- tile_of: int32 [256], replicated, may hold values from 0 to 255, as said below
- upper_rows: bfloat16 [3, 2048, 65536], P(None, 'prow', 'pcol'), may hold values from -0.125 to 0.125
- upper_inv: bfloat16 [3, 2048, 2048], P(None, 'pcol', 'prow'), may hold values from -0.125 to 0.125
- lower_rows: bfloat16 [3, 2048, 65536], P(None, 'prow', 'pcol'), may hold values from -0.125 to 0.125
- lower_inv: bfloat16 [3, 2048, 2048], P(None, 'prow', 'pcol'), may hold values from -0.125 to 0.125
- solved: float32 [64, 65536], P(None, 'pcol'), may hold values from -6 to 6
Outputs:
- forward: float32 [64, 65536], P(None, 'pcol')
- backward: float32 [64, 65536], P(None, 'pcol')
Inputs may be any that keep to these rules, and one draw needn't show every extreme that they name: pivots[p] lies in the same tile of 256 storage columns as p, and each column of a tile appears once. `tile_of`: storage tile d * 256 / 32 + l holds global tile l * 32 + c(d), c a permutation of the process columns.
All inputs are finite; a program needn't handle non-finite values.
Results may differ from a plain program's by a relative error of at most 0.015.
Values may be sent and summed in bfloat16 or wider, within the bound.
No kernel may reach another device: no remote copies, remote signals or barrier semaphores. Data moves between devices by JAX's collectives and lax.ppermute only.
A program may use at most 64 MiB of HBM per device.

v0:
```python
import jax
import jax.numpy as jnp
from jax import lax
from jax.sharding import PartitionSpec as P

NB = 2048
TILE = 256
STEPS = 3


def body(rhs, pivots, tile_of, upper_rows, upper_inv, lower_rows, lower_inv, solved):
    pcol_index = lax.axis_index("pcol")
    prow_index = lax.axis_index("prow")
    width_here = rhs.shape[1]
    tiles_here = width_here // TILE
    tiles_block = NB // TILE
    prow_rows = upper_rows.shape[1]
    count = rhs.shape[0]
    my_tiles = lax.dynamic_slice_in_dim(tile_of, pcol_index * tiles_here, tiles_here)
    my_blocks = my_tiles // tiles_block
    cell_blocks = jnp.repeat(my_blocks, TILE)

    def locate(step):
        match = my_blocks == step
        holds = jnp.any(match)
        tile_slot = jnp.argmax(match)
        block_place = my_tiles[tile_slot] % tiles_block
        return (holds, tile_slot, block_place)

    def write_block(field, block_full, step):
        holds, tile_slot, block_place = locate(step)
        piece = lax.dynamic_slice_in_dim(block_full, block_place * TILE, TILE, 1).astype(
            jnp.float32
        )
        written = lax.dynamic_update_slice_in_dim(field, piece, tile_slot * TILE, 1)
        return jnp.where(holds, written, field)

    state = jnp.take(rhs, pivots - pcol_index * width_here, axis=1)
    finished = []
    for step in range(STEPS):
        holds, tile_slot, block_place = locate(step)
        piece = lax.dynamic_slice_in_dim(state, tile_slot * TILE, TILE, 1)
        piece = jnp.where(holds, piece, 0.0)
        buffer = jnp.zeros((count, NB), jnp.float32)
        buffer = lax.dynamic_update_slice_in_dim(buffer, piece, block_place * TILE, 1)
        block_part = lax.psum_scatter(
            buffer.astype(jnp.bfloat16), "pcol", scatter_dimension=1, tiled=True
        )
        inverse_part = jnp.dot(block_part, upper_inv[step], preferred_element_type=jnp.float32)
        block_rows = lax.psum(inverse_part, "pcol").astype(jnp.bfloat16)
        block_full = lax.all_gather(block_rows, "prow", axis=1, tiled=True)
        update = jnp.dot(block_rows, upper_rows[step], preferred_element_type=jnp.float32)
        total = lax.psum(update, "prow")
        state = state - jnp.where(cell_blocks > step, total, 0.0)
        state = write_block(state, block_full, step)
        finished.append(block_full)
    solution = solved
    for step in reversed(range(STEPS)):
        known = jnp.where(cell_blocks > step, solution, 0.0).astype(jnp.bfloat16)
        partial_value = lax.dot_general(
            known, lower_rows[step], (((1,), (1,)), ((), ())), preferred_element_type=jnp.float32
        )
        sums = lax.psum(partial_value, "pcol")
        own_rows = lax.dynamic_slice_in_dim(
            finished[step], prow_index * prow_rows, prow_rows, 1
        ).astype(jnp.float32)
        resid = (own_rows - sums).astype(jnp.bfloat16)
        inverse_part = jnp.dot(resid, lower_inv[step], preferred_element_type=jnp.float32)
        new_cols = lax.psum(inverse_part, "prow").astype(jnp.bfloat16)
        new_block = lax.all_gather(new_cols, "pcol", axis=1, tiled=True)
        solution = write_block(solution, new_block, step)
    return (state, solution)


def solution(mesh):
    return jax.shard_map(
        body,
        mesh=mesh,
        in_specs=(
            P(None, "pcol"),
            P("pcol"),
            P(),
            P(None, "prow", "pcol"),
            P(None, "pcol", "prow"),
            P(None, "prow", "pcol"),
            P(None, "prow", "pcol"),
            P(None, "pcol"),
        ),
        out_specs=(P(None, "pcol"), P(None, "pcol")),
        check_vma=False,
    )
```

profile of v0, /device:TPU:8, one launch (start us, length us, event | category | flops | bytes accessed | tf_op | source)
XLA Modules:
  0.0 1755.8 jit_solution(12627563569382211011)
XLA Ops:
  7.2 1.0 copy.45
  8.3 0.8 broadcast_compare_fusion
  9.0 0.7 compare_reduce_fusion
  11.0 0.7 compare_reduce_fusion.4
  13.1 0.7 compare_reduce_fusion.2
  17.1 1.4 fusion.55
  20.4 0.7 fusion.51
  21.2 0.7 compare_and_fusion
  22.6 0.7 compare_reduce_fusion.1
  23.3 1.4 copy.12
  24.7 5.5 gather_fusion
  30.2 0.3 copy.13
  30.6 0.7 bitcast_dynamic-update-slice_fusion
  31.3 1.0 copy.20
  32.3 215.0 %reduce-scatter.10.cloned.1.call-done = bf16[64,64]{1,0:T(8,128)(2,1)} async-done(((bf16[2048,64]{1,0:T(8,128)(2,1)}), bf16[64,64]{1,0:T(8,128)(2,1)}) %reduce-scatter.10.cloned.1.call-update) | async-done | bytes 8208
  247.3 0.9 fusion.34
  248.2 136.2 %psum.84 = bf16[64,256]{1,0:T(8,128)(2,1)S(1)} all-reduce(f32[64,256]{1,0:T(8,128)S(1)} %fusion.34), channel_id=1, replica_groups=mesh['prow'=8,'pcol'=32] {'pcol'}, use_global_device_ids=true, to_apply=%region_3.4 | all-reduce | flops 16384 | bytes 98304 | tf_op jit(solution)/shard_map/psum | solution.py:50
  384.4 2.3 fusion.10
  389.3 13.2 all_gather.18
  402.5 52.6 %all-reduce.7.cloned.1.call-done = f32[64,2048]{1,0:T(8,128)} async-done(((f32[64,2048]{1,0:T(8,128)}), f32[64,2048]{1,0:T(8,128)}) %all-reduce.7.cloned.1.call-update) | async-done | bytes 524304 | tf_op jit(solution)/shard_map/psum | solution.py:53
  455.1 1.1 bitcast_subtract_fusion
  456.2 0.7 select_dynamic-update-slice_fusion.7
  456.9 0.7 select_dynamic-update-slice_fusion.6
  457.6 1.0 copy.22
  458.7 212.1 %reduce-scatter.12.cloned.1.call-done = bf16[64,64]{1,0:T(8,128)(2,1)} async-done(((bf16[2048,64]{1,0:T(8,128)(2,1)}), bf16[64,64]{1,0:T(8,128)(2,1)}) %reduce-scatter.12.cloned.1.call-update) | async-done | bytes 8208
  670.8 0.9 fusion.32
  671.7 136.1 %psum.86 = bf16[64,256]{1,0:T(8,128)(2,1)S(1)} all-reduce(f32[64,256]{1,0:T(8,128)S(1)} %fusion.32), channel_id=1, replica_groups=mesh['prow'=8,'pcol'=32] {'pcol'}, use_global_device_ids=true, to_apply=%region_8.9 | all-reduce | flops 16384 | bytes 98304 | tf_op jit(solution)/shard_map/psum | solution.py:50
  807.8 2.3 fusion.8
  812.6 13.1 all_gather.19
  825.8 52.8 %all-reduce.9.cloned.1.call-done = f32[64,2048]{1,0:T(8,128)} async-done(((f32[64,2048]{1,0:T(8,128)}), f32[64,2048]{1,0:T(8,128)}) %all-reduce.9.cloned.1.call-update) | async-done | bytes 524304 | tf_op jit(solution)/shard_map/psum | solution.py:53
  878.6 1.1 select_subtract_fusion.1
  879.7 0.7 select_dynamic-update-slice_fusion.5
  880.4 0.6 select_dynamic-update-slice_fusion.4
  881.0 1.0 copy.24
  882.2 2.3 fusion.4
  884.6 209.7 %reduce-scatter.14.cloned.1.call-done = bf16[64,64]{1,0:T(8,128)(2,1)} async-done(((bf16[2048,64]{1,0:T(8,128)(2,1)}), bf16[64,64]{1,0:T(8,128)(2,1)}) %reduce-scatter.14.cloned.1.call-update) | async-done | bytes 8208
  1094.3 0.9 fusion.30
  1095.2 136.1 %psum.88 = bf16[64,256]{1,0:T(8,128)(2,1)S(1)} all-reduce(f32[64,256]{1,0:T(8,128)S(1)} %fusion.30), channel_id=1, replica_groups=mesh['prow'=8,'pcol'=32] {'pcol'}, use_global_device_ids=true, to_apply=%region_13.14 | all-reduce | flops 16384 | bytes 98304 | tf_op jit(solution)/shard_map/psum | solution.py:50
  1231.3 13.1 all_gather.20
  1244.5 1.0 fusion.24
  1245.4 25.8 %psum.91 = bf16[64,64]{1,0:T(8,128)(2,1)S(1)} all-reduce(f32[64,64]{1,0:T(8,128)S(1)} %fusion.24), channel_id=1, replica_groups=mesh['prow'=8,'pcol'=32] {'prow'}, use_global_device_ids=true, to_apply=%region_16.17 | all-reduce | flops 4096 | bytes 24576 | tf_op jit(solution)/shard_map/psum | solution.py:69
  1271.2 0.1 copy.14
  1271.3 51.7 %all_gather.21 = bf16[64,2048]{0,1:T(8,128)(2,1)S(1)} all-gather(bf16[64,64]{0,1:T(8,128)(2,1)S(1)} %copy.14), channel_id=1, replica_groups=mesh['prow'=8,'pcol'=32] {'pcol'}, dimensions={1}, use_global_device_ids=true | all-gather | bytes 270336 | tf_op jit(solution)/shard_map/all_gather | solution.py:70
  1323.1 0.1 copy.26
  1323.2 0.6 select_dynamic-update-slice_fusion.2
  1323.7 2.3 fusion.2
  1326.1 136.4 %all-reduce.15.cloned.1.call-done = f32[64,256]{1,0:T(8,128)} async-done(((f32[64,256]{1,0:T(8,128)}), f32[64,256]{1,0:T(8,128)}) %all-reduce.15.cloned.1.call-update) | async-done | bytes 65552 | tf_op jit(solution)/shard_map/psum | solution.py:63
  1462.5 1.0 fusion.25
  1463.4 23.6 %psum.93 = bf16[64,64]{1,0:T(8,128)(2,1)S(1)} all-reduce(f32[64,64]{1,0:T(8,128)S(1)} %fusion.25), channel_id=1, replica_groups=mesh['prow'=8,'pcol'=32] {'prow'}, use_global_device_ids=true, to_apply=%region_18.19 | all-reduce | flops 4096 | bytes 24576 | tf_op jit(solution)/shard_map/psum | solution.py:69
  1487.1 0.1 copy.16
  1487.2 47.4 %all_gather.22 = bf16[64,2048]{0,1:T(8,128)(2,1)S(1)} all-gather(bf16[64,64]{0,1:T(8,128)(2,1)S(1)} %copy.16), channel_id=1, replica_groups=mesh['prow'=8,'pcol'=32] {'pcol'}, dimensions={1}, use_global_device_ids=true | all-gather | bytes 270336 | tf_op jit(solution)/shard_map/all_gather | solution.py:70
  1534.6 0.1 copy.27
  1534.7 0.7 select_dynamic-update-slice_fusion.1
  1535.4 2.3 fusion
  1537.8 2.3 fusion.6
  1540.1 133.5 %all-reduce.17.cloned.1.call-done = f32[64,256]{1,0:T(8,128)} async-done(((f32[64,256]{1,0:T(8,128)}), f32[64,256]{1,0:T(8,128)}) %all-reduce.17.cloned.1.call-update) | async-done | bytes 65552 | tf_op jit(solution)/shard_map/psum | solution.py:63
  1673.7 1.0 fusion.26
  1674.6 23.6 %psum.95 = bf16[64,64]{1,0:T(8,128)(2,1)S(1)} all-reduce(f32[64,64]{1,0:T(8,128)S(1)} %fusion.26), channel_id=1, replica_groups=mesh['prow'=8,'pcol'=32] {'prow'}, use_global_device_ids=true, to_apply=%region_20.21 | all-reduce | flops 4096 | bytes 24576 | tf_op jit(solution)/shard_map/psum | solution.py:69
  1698.2 0.1 copy.18
  1698.3 47.5 %all_gather.23 = bf16[64,2048]{0,1:T(8,128)(2,1)S(1)} all-gather(bf16[64,64]{0,1:T(8,128)(2,1)S(1)} %copy.18), channel_id=1, replica_groups=mesh['prow'=8,'pcol'=32] {'pcol'}, dimensions={1}, use_global_device_ids=true | all-gather | bytes 270336 | tf_op jit(solution)/shard_map/all_gather | solution.py:70
  1745.9 0.7 select_dynamic-update-slice_fusion
  1746.6 1.3 select_subtract_fusion
  1747.9 0.6 select_dynamic-update-slice_fusion.3
  1748.5 0.8 copy-done.1
  (41 shorter events, 1.0 us)
Async XLA Ops:
  7.2 240.1 %reduce-scatter.10.cloned.1.call-start = ((), (), s32[]{:S(2)}) async-start(), calls=%async_computation.9 | async-start | bytes 540672
  30.1 217.2 %copy-start.2 = (bf16[3,64,256]{2,1,0:T(8,128)(2,1)S(1)}, bf16[3,64,256]{2,1,0:T(8,128)(2,1)}, u32[]{:S(2)}) copy-start(bf16[3,64,256]{2,1,0:T(8,128)(2,1)} %param.12) | copy-start | bytes 294916
  32.3 422.8 %all-reduce.7.cloned.1.call-start = ((), (), s32[]{:S(2)}) async-start(), calls=%async_computation.3 | async-start | bytes 1048576 | tf_op jit(solution)/shard_map/psum | solution.py:53
  386.7 284.1 %reduce-scatter.12.cloned.1.call-start = ((), (), s32[]{:S(2)}) async-start(), calls=%async_computation.10 | async-start | bytes 540672
  458.7 419.9 %all-reduce.9.cloned.1.call-start = ((), (), s32[]{:S(2)}) async-start(), calls=%async_computation.4 | async-start | bytes 1048576 | tf_op jit(solution)/shard_map/psum | solution.py:53
  810.1 434.4 %copy-start.3 = (bf16[3,256,64]{1,2,0:T(8,128)(2,1)S(1)}, bf16[3,256,64]{1,2,0:T(8,128)(2,1)}, u32[]{:S(2)}) copy-start(bf16[3,256,64]{1,2,0:T(8,128)(2,1)} %param.14) | copy-start | bytes 294916
  810.1 284.2 %reduce-scatter.14.cloned.1.call-start = ((), (), s32[]{:S(2)}) async-start(), calls=%async_computation.11 | async-start | bytes 540672
  882.0 362.4 %all-reduce.13.cloned.1.call-start = ((), (), s32[]{:S(2)}) async-start(), calls=%async_computation.6 | async-start | bytes 131072 | tf_op jit(solution)/shard_map/psum | solution.py:63
  884.5 578.0 %all-reduce.15.cloned.1.call-start = ((), (), s32[]{:S(2)}) async-start(), calls=%async_computation.7 | async-start | bytes 131072 | tf_op jit(solution)/shard_map/psum | solution.py:63
  1326.1 347.6 %all-reduce.17.cloned.1.call-start = ((), (), s32[]{:S(2)}) async-start(), calls=%async_computation.8 | async-start | bytes 131072 | tf_op jit(solution)/shard_map/psum | solution.py:63
  1537.7 208.9 %all-reduce.11.cloned.1.call-start = ((), (), s32[]{:S(2)}) async-start(), calls=%async_computation.5 | async-start | bytes 1048576 | tf_op jit(solution)/shard_map/psum | solution.py:53
  1746.6 1.9 copy-start
  1748.5 0.8 copy-start.1
Sparse Core Ops, SparseCore 0:
  32.4 214.8 reduce-scatter.9
  386.8 68.2 all-reduce.6
  459.5 211.2 reduce-scatter.11
  810.3 68.2 all-reduce.8
  882.8 211.4 reduce-scatter.13
  1098.6 138.1 all-reduce.12
  1326.2 136.2 all-reduce.14
  1537.8 135.7 all-reduce.16
  1676.7 64.1 all-reduce.10
where the time goes:
time: 1760 us
  waiting for transfers between devices  1010 us (57%)
  blocking collectives  667 us (38%)
  between operations  27.6 us (2%)
  matrix products  19.4 us (1%)
    unnamed x12, waiting for transfers between devices  637 us
    psum x3, blocking collectives, body(): block_rows = lax.psum(inverse_part, 'pcol').astype(jnp.bfloat16)  408 us
    psum x3, waiting for transfers between devices, body(): sums = lax.psum(partial_value, 'pcol')  270 us
    all_gather x3, blocking collectives, body(): new_block = lax.all_gather(new_cols, 'pcol', axis=1, tiled=True)  147 us
    psum x3, waiting for transfers between devices, body(): total = lax.psum(update, 'prow')  105 us
    psum x3, blocking collectives, body(): new_cols = lax.psum(inverse_part, 'prow').astype(jnp.bfloat16)  73 us
    all_gather x3, blocking collectives, body(): block_full = lax.all_gather(block_rows, 'prow', axis=1, tiled=True)  39.4 us
  transfers between devices with their start and end apart: 9, of which 7 were waited for; matrix products, arithmetic and copies ran while one was open for 0% of the time, Pallas kernels for 0%

commit v1 on v0

--- a/solution.py
+++ b/solution.py
@@ -67,7 +67,9 @@
         resid = (own_rows - sums).astype(jnp.bfloat16)
         inverse_part = jnp.dot(resid, lower_inv[step], preferred_element_type=jnp.float32)
         new_cols = lax.psum(inverse_part, "prow").astype(jnp.bfloat16)
-        new_block = lax.all_gather(new_cols, "pcol", axis=1, tiled=True)
+        new_block = jnp.concatenate(
+            lax.all_to_all(jnp.stack([new_cols] * lax.axis_size("pcol")), "pcol", 0, 0), axis=1
+        )
         solution = write_block(solution, new_block, step)
     return (state, solution)
 

time: 1760 us -> 1690 us (0.960)
  blocking collectives: 667 us -> 559 us
  waiting for transfers between devices: 1010 us -> 1040 us
    all_gather x3 -> x0, blocking collectives: 147 us -> none  [body(): new_block = lax.all_gather(new_cols, 'pcol', axis=1, tiled=True)]
    all_to_all x0 -> x2, blocking collectives: none -> 37.8 us  [body(): lax.all_to_all(jnp.stack([new_cols] * lax.axis_size('pcol')), 'pcol', 0, 0)]
    psum x3, waiting for transfers between devices: 105 us -> 139 us  [body(): total = lax.psum(update, 'prow')]
  transfers between devices with their start and end apart: 9 -> 10, of which waited for: 7 -> 8; matrix products, arithmetic and copies ran while one was open for 0% -> 1% of each run, Pallas kernels for 0% -> 0%
where the time goes in v1:
time: 1690 us
  waiting for transfers between devices  1040 us (62%)
  blocking collectives  559 us (33%)
  between operations  27.6 us (2%)
  local copies, waits for them, and re-layouts  19.4 us (1%)
  matrix products  19.4 us (1%)
    unnamed x12, waiting for transfers between devices  637 us
    psum x3, blocking collectives, body(): block_rows = lax.psum(inverse_part, 'pcol').astype(jnp.bfloat16)  408 us
    psum x3, waiting for transfers between devices, body(): sums = lax.psum(partial_value, 'pcol')  266 us
    psum x3, waiting for transfers between devices, body(): total = lax.psum(update, 'prow')  139 us
    psum x3, blocking collectives, body(): new_cols = lax.psum(inverse_part, 'prow').astype(jnp.bfloat16)  73.2 us
    all_gather x3, blocking collectives, body(): block_full = lax.all_gather(block_rows, 'prow', axis=1, tiled=True)  39.4 us
    all_to_all x2, blocking collectives, body(): lax.all_to_all(jnp.stack([new_cols] * lax.axis_size('pcol')), 'pcol', 0, 0)  37.8 us
  transfers between devices with their start and end apart: 10, of which 8 were waited for; matrix products, arithmetic and copies ran while one was open for 1% of the time, Pallas kernels for 0%

profile of v1, /device:TPU:8, one launch (start us, length us, event | category | flops | bytes accessed | tf_op | source)
XLA Modules:
  0.0 1689.4 jit_solution(78561630815423263)
XLA Ops:
  7.2 1.0 copy.39
  8.3 0.8 broadcast_compare_fusion
  9.0 0.7 compare_reduce_fusion
  11.0 0.7 compare_reduce_fusion.4
  13.1 0.7 compare_reduce_fusion.2
  17.1 1.4 fusion.55
  20.4 0.7 fusion.51
  21.2 0.7 compare_and_fusion
  22.6 0.7 compare_reduce_fusion.1
  23.3 1.4 copy.12
  24.7 5.5 gather_fusion
  30.6 0.6 bitcast_dynamic-update-slice_fusion
  31.2 1.0 copy.17
  32.3 215.0 %reduce-scatter.10.cloned.1.call-done = bf16[64,64]{1,0:T(8,128)(2,1)} async-done(((bf16[2048,64]{1,0:T(8,128)(2,1)}), bf16[64,64]{1,0:T(8,128)(2,1)}) %reduce-scatter.10.cloned.1.call-update) | async-done | bytes 8208
  247.3 0.9 fusion.34
  248.2 136.2 %psum.84 = bf16[64,256]{1,0:T(8,128)(2,1)S(1)} all-reduce(f32[64,256]{1,0:T(8,128)S(1)} %fusion.34), channel_id=1, replica_groups=mesh['prow'=8,'pcol'=32] {'pcol'}, use_global_device_ids=true, to_apply=%region_3.4 | all-reduce | flops 16384 | bytes 98304 | tf_op jit(solution)/shard_map/psum | solution.py:50
  384.3 2.3 fusion.10
  389.3 13.2 all_gather.9
  402.4 52.6 %all-reduce.7.cloned.1.call-done = f32[64,2048]{1,0:T(8,128)} async-done(((f32[64,2048]{1,0:T(8,128)}), f32[64,2048]{1,0:T(8,128)}) %all-reduce.7.cloned.1.call-update) | async-done | bytes 524304 | tf_op jit(solution)/shard_map/psum | solution.py:53
  455.0 1.1 bitcast_subtract_fusion
  456.1 0.7 select_dynamic-update-slice_fusion.7
  456.8 0.7 select_dynamic-update-slice_fusion.6
  457.5 1.0 copy.19
  458.6 212.1 %reduce-scatter.12.cloned.1.call-done = bf16[64,64]{1,0:T(8,128)(2,1)} async-done(((bf16[2048,64]{1,0:T(8,128)(2,1)}), bf16[64,64]{1,0:T(8,128)(2,1)}) %reduce-scatter.12.cloned.1.call-update) | async-done | bytes 8208
  670.8 0.9 fusion.32
  671.7 136.1 %psum.86 = bf16[64,256]{1,0:T(8,128)(2,1)S(1)} all-reduce(f32[64,256]{1,0:T(8,128)S(1)} %fusion.32), channel_id=1, replica_groups=mesh['prow'=8,'pcol'=32] {'pcol'}, use_global_device_ids=true, to_apply=%region_8.9 | all-reduce | flops 16384 | bytes 98304 | tf_op jit(solution)/shard_map/psum | solution.py:50
  807.7 2.3 fusion.8
  812.6 13.1 all_gather.10
  825.7 52.8 %all-reduce.9.cloned.1.call-done = f32[64,2048]{1,0:T(8,128)} async-done(((f32[64,2048]{1,0:T(8,128)}), f32[64,2048]{1,0:T(8,128)}) %all-reduce.9.cloned.1.call-update) | async-done | bytes 524304 | tf_op jit(solution)/shard_map/psum | solution.py:53
  878.6 1.1 select_subtract_fusion.1
  879.7 0.7 select_dynamic-update-slice_fusion.5
  880.4 0.6 select_dynamic-update-slice_fusion.4
  881.0 1.0 copy.21
  882.1 2.3 fusion.4
  884.5 209.7 %reduce-scatter.14.cloned.1.call-done = bf16[64,64]{1,0:T(8,128)(2,1)} async-done(((bf16[2048,64]{1,0:T(8,128)(2,1)}), bf16[64,64]{1,0:T(8,128)(2,1)}) %reduce-scatter.14.cloned.1.call-update) | async-done | bytes 8208
  1094.3 0.9 fusion.30
  1095.2 136.1 %psum.88 = bf16[64,256]{1,0:T(8,128)(2,1)S(1)} all-reduce(f32[64,256]{1,0:T(8,128)S(1)} %fusion.30), channel_id=1, replica_groups=mesh['prow'=8,'pcol'=32] {'pcol'}, use_global_device_ids=true, to_apply=%region_13.14 | all-reduce | flops 16384 | bytes 98304 | tf_op jit(solution)/shard_map/psum | solution.py:50
  1231.3 13.1 all_gather.11
  1244.4 1.0 fusion.24
  1245.4 25.8 %psum.91 = bf16[64,64]{1,0:T(8,128)(2,1)S(1)} all-reduce(f32[64,64]{1,0:T(8,128)S(1)} %fusion.24), channel_id=1, replica_groups=mesh['prow'=8,'pcol'=32] {'prow'}, use_global_device_ids=true, to_apply=%region_16.17 | all-reduce | flops 4096 | bytes 24576 | tf_op jit(solution)/shard_map/psum | solution.py:69
  1271.3 0.4 reshape.61
  1271.7 21.0 %all_to_all.15 = bf16[32,2,2048]{2,1,0:T(2,128)(2,1)S(1)} all-to-all(bf16[32,2,2048]{2,1,0:T(2,128)(2,1)S(1)} %reshape.61), channel_id=1, replica_groups=mesh['prow'=8,'pcol'=32] {'pcol'}, dimensions={0} | all-to-all | bytes 524288 | tf_op jit(solution)/shard_map/all_to_all | solution.py:71
  1293.4 0.5 reshape.41
  1293.9 0.6 select_dynamic-update-slice_fusion.2
  1294.4 2.3 fusion.2
  1296.8 134.3 %all-reduce.15.cloned.1.call-done = f32[64,256]{1,0:T(8,128)} async-done(((f32[64,256]{1,0:T(8,128)}), f32[64,256]{1,0:T(8,128)}) %all-reduce.15.cloned.1.call-update) | async-done | bytes 65552 | tf_op jit(solution)/shard_map/psum | solution.py:63
  1431.1 1.0 fusion.25
  1432.1 23.6 %psum.93 = bf16[64,64]{1,0:T(8,128)(2,1)S(1)} all-reduce(f32[64,64]{1,0:T(8,128)S(1)} %fusion.25), channel_id=1, replica_groups=mesh['prow'=8,'pcol'=32] {'prow'}, use_global_device_ids=true, to_apply=%region_18.19 | all-reduce | flops 4096 | bytes 24576 | tf_op jit(solution)/shard_map/psum | solution.py:69
  1456.2 16.8 all_to_all.16
  1473.7 0.5 reshape.43
  1474.1 0.7 select_dynamic-update-slice_fusion.1
  1474.8 2.3 fusion
  1477.2 2.3 fusion.6
  1479.6 131.8 %all-reduce.17.cloned.1.call-done = f32[64,256]{1,0:T(8,128)} async-done(((f32[64,256]{1,0:T(8,128)}), f32[64,256]{1,0:T(8,128)}) %all-reduce.17.cloned.1.call-update) | async-done | bytes 65552 | tf_op jit(solution)/shard_map/psum | solution.py:63
  1611.4 1.0 fusion.26
  1612.3 23.8 %psum.95 = bf16[64,64]{1,0:T(8,128)(2,1)S(1)} all-reduce(f32[64,64]{1,0:T(8,128)S(1)} %fusion.26), channel_id=1, replica_groups=mesh['prow'=8,'pcol'=32] {'prow'}, use_global_device_ids=true, to_apply=%region_20.21 | all-reduce | flops 4096 | bytes 24576 | tf_op jit(solution)/shard_map/psum | solution.py:69
  1636.2 1.1 reshape.65
  1637.3 7.2 all-to-all-start.2
  1644.5 34.0 %all-reduce.11.cloned.1.call-done = f32[64,2048]{1,0:T(8,128)} async-done(((f32[64,2048]{1,0:T(8,128)}), f32[64,2048]{1,0:T(8,128)}) %all-reduce.11.cloned.1.call-update) | async-done | bytes 524304 | tf_op jit(solution)/shard_map/psum | solution.py:53
  1678.5 1.1 select_subtract_fusion
  1679.6 0.6 select_dynamic-update-slice_fusion.3
  1680.9 0.5 reshape.45
  1681.4 0.7 select_dynamic-update-slice_fusion
  1682.1 0.8 copy-done
  (48 shorter events, 4.0 us)
Async XLA Ops:
  7.2 240.1 %reduce-scatter.10.cloned.1.call-start = ((), (), s32[]{:S(2)}) async-start(), calls=%async_computation.12 | async-start | bytes 540672
  30.1 217.1 %copy-start.2 = (bf16[3,64,256]{2,1,0:T(8,128)(2,1)S(1)}, bf16[3,64,256]{2,1,0:T(8,128)(2,1)}, u32[]{:S(2)}) copy-start(bf16[3,64,256]{2,1,0:T(8,128)(2,1)} %param.12) | copy-start | bytes 294916
  32.2 422.8 %all-reduce.7.cloned.1.call-start = ((), (), s32[]{:S(2)}) async-start(), calls=%async_computation.6 | async-start | bytes 1048576 | tf_op jit(solution)/shard_map/psum | solution.py:53
  386.7 284.1 %reduce-scatter.12.cloned.1.call-start = ((), (), s32[]{:S(2)}) async-start(), calls=%async_computation.13 | async-start | bytes 540672
  458.6 420.0 %all-reduce.9.cloned.1.call-start = ((), (), s32[]{:S(2)}) async-start(), calls=%async_computation.7 | async-start | bytes 1048576 | tf_op jit(solution)/shard_map/psum | solution.py:53
  810.1 434.4 %copy-start.3 = (bf16[3,256,64]{1,2,0:T(8,128)(2,1)S(1)}, bf16[3,256,64]{1,2,0:T(8,128)(2,1)}, u32[]{:S(2)}) copy-start(bf16[3,256,64]{1,2,0:T(8,128)(2,1)} %param.14) | copy-start | bytes 294916
  810.1 284.2 %reduce-scatter.14.cloned.1.call-start = ((), (), s32[]{:S(2)}) async-start(), calls=%async_computation.14 | async-start | bytes 540672
  882.0 362.4 %all-reduce.13.cloned.1.call-start = ((), (), s32[]{:S(2)}) async-start(), calls=%async_computation.9 | async-start | bytes 131072 | tf_op jit(solution)/shard_map/psum | solution.py:63
  884.5 546.6 %all-reduce.15.cloned.1.call-start = ((), (), s32[]{:S(2)}) async-start(), calls=%async_computation.10 | async-start | bytes 131072 | tf_op jit(solution)/shard_map/psum | solution.py:63
  1296.8 314.6 %all-reduce.17.cloned.1.call-start = ((), (), s32[]{:S(2)}) async-start(), calls=%async_computation.11 | async-start | bytes 131072 | tf_op jit(solution)/shard_map/psum | solution.py:63
  1477.2 201.4 %all-reduce.11.cloned.1.call-start = ((), (), s32[]{:S(2)}) async-start(), calls=%async_computation.8 | async-start | bytes 1048576 | tf_op jit(solution)/shard_map/psum | solution.py:53
  1637.3 42.9 %all-to-all-start.2 = ((bf16[32,2,2048]{2,1,0:T(2,128)(2,1)}), bf16[32,2,2048]{2,1,0:T(2,128)(2,1)S(1)}, u32[]{:S(2)}, u32[]{:S(2)}) async-start(bf16[32,2,2048]{2,1,0:T(2,128)(2,1)} %reshape.65), calls=%async_computation.2 | async-start | bytes 524288 | tf_op jit(solution)/shard_map/all_to_all | solution.py:71
  1680.2 1.9 copy-start.1
  1682.1 0.8 copy-start
Sparse Core Ops, SparseCore 0:
  32.4 214.8 reduce-scatter.9
  386.8 68.2 all-reduce.6
  459.4 211.2 reduce-scatter.11
  810.2 68.2 all-reduce.8
  882.8 211.4 reduce-scatter.13
  1098.5 138.1 all-reduce.12
  1296.9 134.1 all-reduce.14
  1477.3 134.0 all-reduce.16
  1614.4 64.1 all-reduce.10
